TPU v7x, 256 devices: a whole 4x4x8 slice. The times are simulated.
256 devices in a mesh: seq: 64 (over x, z, core), tp: 4 (over y).
Axes of the slice: x: 4, y: 4, z: 8, core: 2. Of those that a mesh axis runs over, the one named last changes fastest.
Arguments:
- hidden_in: bfloat16 [256, 2048], P('seq'), may hold values from -6 to 6
- query_weight: bfloat16 [2048, 2048], P(None, 'tp'), may hold values from -0.125 to 0.125
- key_weight: bfloat16 [2048, 2048], P(None, 'tp'), may hold values from -0.125 to 0.125
- value_weight: bfloat16 [2048, 2048], P(None, 'tp'), may hold values from -0.125 to 0.125
- out_weight: bfloat16 [2048, 2048], P('tp'), may hold values from -0.125 to 0.125
- query_gain: float32 [2048], P('tp'), may hold values from 0.5 to 1.5
- key_gain: float32 [2048], P('tp'), may hold values from 0.5 to 1.5
- post_gain: float32 [2048], P('tp'), may hold values from 0.5 to 1.5
- key_cache: bfloat16 [4, 8192, 2048], P(None, 'seq', 'tp'), may hold values from -110 to 110
- value_cache: bfloat16 [4, 8192, 2048], P(None, 'seq', 'tp'), may hold values from -6 to 6
- cache_lengths: int32 [4], replicated, may hold values from 1024 to 8128
- parents: int32 [4, 64], replicated, may hold values from -1 to 62, as said below
- accepted_leaf: int32 [4], replicated, may hold values from 0 to 63
Outputs:
- hidden_out: bfloat16 [256, 2048], P('seq', 'tp')
- new_key_cache: bfloat16 [4, 8192, 2048], P(None, 'seq', 'tp')
- new_value_cache: bfloat16 [4, 8192, 2048], P(None, 'seq', 'tp')
Inputs may be any that keep to these rules, and one draw needn't show every extreme that they name: parents[r, 0] = -1; for i >= 1, parents[r, i] lies in max(0, i - 3) to i - 1; parents[r, 63] = 62.
All inputs are finite; a program needn't handle non-finite values.
Results may differ from a plain program's by a relative error of at most 0.019.
Values may be sent and summed in bfloat16 or wider, within the bound.
A program may use at most 128 MiB of HBM per device.

v0:
```python
import math
import jax
import jax.numpy as jnp
from jax import lax
from jax.sharding import PartitionSpec as P

HEAD_DIM = 128
EPS = 1e-06
THETA = 500000.0
NEG = -1e30


def joined_2(x, axis, combine):
    everything = jax.tree.map(lambda part: lax.all_gather(part, axis), x)
    initial = jax.tree.map(lambda part: part[0], everything)

    def step(k, so_far):
        return combine(so_far, jax.tree.map(lambda part: part[k], everything))

    return lax.fori_loop(1, lax.axis_size(axis), step, initial)


def ancestry(parents):
    number = parents.shape[-1]
    columns = jnp.arange(number, dtype=jnp.int32)
    single = (parents[:, :, None] == columns[None, None, :]).astype(jnp.float32)
    ancestors = jnp.eye(number, dtype=jnp.float32)[None] + single
    for repeat in range(max(1, (number - 1).bit_length())):
        ancestors = jnp.minimum(
            jnp.einsum("rij,rjk->rik", ancestors, ancestors, precision=lax.Precision.HIGHEST), 1.0
        )
    tree_depth = jnp.sum(ancestors, axis=-1) - 1.0
    return (ancestors, tree_depth)


def rotary(values, positions):
    half_dim = values.shape[-1] // 2
    freqs = THETA ** (-2.0 * jnp.arange(half_dim, dtype=jnp.float32) / values.shape[-1])
    angles = positions[:, None, None] * freqs[None, None, :]
    cosine = jnp.cos(angles)
    sine = jnp.sin(angles)
    first = values[..., :half_dim]
    second = values[..., half_dim:]
    return jnp.concatenate(
        [first * cosine - second * sine, second * cosine + first * sine], axis=-1
    )


def prepare(raw, square_sum, gain, positions, width_all):
    scaled = raw * lax.rsqrt(square_sum / width_all + EPS)[:, None] * gain[None, :]
    rows_here = raw.shape[0]
    heads_here = raw.shape[1] // HEAD_DIM
    turned = rotary(scaled.reshape(rows_here, heads_here, HEAD_DIM), positions)
    return turned.reshape(rows_here, heads_here * HEAD_DIM).astype(jnp.bfloat16)


def join_partials(first, second):
    peak_first, total_first, out_first = first
    peak_second, total_second, out_second = second
    highest = jnp.maximum(peak_first, peak_second)
    scale_first = jnp.exp(peak_first - highest)
    scale_second = jnp.exp(peak_second - highest)
    rows_here, heads_here = highest.shape
    joined = (
        out_first.reshape(rows_here, heads_here, -1) * scale_first[..., None]
        + out_second.reshape(rows_here, heads_here, -1) * scale_second[..., None]
    )
    return (
        highest,
        total_first * scale_first + total_second * scale_second,
        joined.reshape(out_first.shape),
    )


def body(
    hidden_in,
    query_weight,
    key_weight,
    value_weight,
    out_weight,
    query_gain,
    key_gain,
    post_gain,
    key_cache,
    value_cache,
    cache_lengths,
    parents,
    accepted_leaf,
):
    requests, block, local_width = key_cache.shape
    draft = parents.shape[1]
    tokens = requests * draft
    own_rows = hidden_in.shape[0]
    model_width = hidden_in.shape[1]
    heads_here = local_width // HEAD_DIM
    full_width = local_width * lax.axis_size("tp")
    seq_index = lax.axis_index("seq")
    tp_index = lax.axis_index("tp")
    row_start = seq_index * own_rows
    ancestors, tree_depth = ancestry(parents)
    positions = (cache_lengths[:, None].astype(jnp.float32) + tree_depth).reshape(tokens)
    piece = lax.all_gather(hidden_in, "seq", axis=0, tiled=True)
    raw = jnp.concatenate(
        [
            jnp.dot(piece, query_weight, preferred_element_type=jnp.float32),
            jnp.dot(piece, key_weight, preferred_element_type=jnp.float32),
            jnp.dot(piece, value_weight, preferred_element_type=jnp.float32),
        ],
        axis=1,
    )
    query_raw = raw[:, :local_width]
    key_raw = raw[:, local_width : 2 * local_width]
    value_raw = raw[:, 2 * local_width :]
    query_square, key_square = lax.psum(
        (jnp.sum(query_raw * query_raw, axis=1), jnp.sum(key_raw * key_raw, axis=1)), "tp"
    )
    queries = prepare(query_raw, query_square, query_gain, positions, full_width)
    keys = prepare(key_raw, key_square, key_gain, positions, full_width)
    values = value_raw.astype(jnp.bfloat16)
    factor = 1.0 / math.sqrt(HEAD_DIM)
    query_blocks = queries.reshape(requests, draft, heads_here, HEAD_DIM)
    cache_keys = key_cache.reshape(requests, block, heads_here, HEAD_DIM)
    cache_values = value_cache.reshape(requests, block, heads_here, HEAD_DIM)
    places = seq_index * block + jnp.arange(block, dtype=jnp.int32)
    cache_scores = (
        jnp.einsum("rihd,rlhd->rihl", query_blocks, cache_keys, preferred_element_type=jnp.float32)
        * factor
    )
    visible = (places[None, :] < cache_lengths[:, None])[:, None, None, :]
    cache_scores = jnp.where(visible, cache_scores, NEG)
    cache_peak = jnp.max(cache_scores, axis=-1)
    cache_weights = jnp.where(visible, jnp.exp(cache_scores - cache_peak[..., None]), 0.0)
    cache_total = jnp.sum(cache_weights, axis=-1).reshape(tokens, heads_here)
    cache_out = jnp.einsum(
        "rihl,rlhd->rihd",
        cache_weights,
        cache_values.astype(jnp.float32),
        precision=lax.Precision.HIGHEST,
    ).reshape(tokens, local_width)
    cache_peak = cache_peak.reshape(tokens, heads_here)
    request_now = row_start // draft
    own_queries_all = lax.dynamic_slice_in_dim(queries, row_start, own_rows).reshape(
        own_rows, heads_here, HEAD_DIM
    )
    request_keys = lax.dynamic_index_in_dim(
        keys.reshape(requests, draft, local_width), request_now, 0, keepdims=False
    ).reshape(draft, heads_here, HEAD_DIM)
    request_values = lax.dynamic_index_in_dim(
        values.reshape(requests, draft, local_width), request_now, 0, keepdims=False
    ).reshape(draft, heads_here, HEAD_DIM)
    tree_rows = lax.dynamic_slice_in_dim(ancestors.reshape(tokens, draft), row_start, own_rows)
    draft_scores = (
        jnp.einsum(
            "ihd,jhd->ihj", own_queries_all, request_keys, preferred_element_type=jnp.float32
        )
        * factor
    )
    tree_mask = (tree_rows > 0.5)[:, None, :]
    draft_scores = jnp.where(tree_mask, draft_scores, NEG)
    draft_peak = jnp.max(draft_scores, axis=-1)
    draft_weights = jnp.where(tree_mask, jnp.exp(draft_scores - draft_peak[..., None]), 0.0)
    draft_total = jnp.sum(draft_weights, axis=-1)
    draft_out = jnp.einsum(
        "ihj,jhd->ihd",
        draft_weights,
        request_values.astype(jnp.float32),
        precision=lax.Precision.HIGHEST,
    ).reshape(own_rows, local_width)
    merged = joined_2((cache_peak, cache_total, cache_out), "seq", join_partials)
    mine = tuple((lax.dynamic_slice_in_dim(member, row_start, own_rows) for member in merged))
    highest, denominator, summed = join_partials(mine, (draft_peak, draft_total, draft_out))
    attention = (
        (summed.reshape(own_rows, heads_here, HEAD_DIM) / denominator[..., None])
        .reshape(own_rows, local_width)
        .astype(jnp.bfloat16)
    )
    projected = jnp.dot(attention, out_weight, preferred_element_type=jnp.float32)
    feature_count = model_width // lax.axis_size("tp")
    summed_heads = lax.psum(projected, "tp")
    power = jnp.sum(summed_heads * summed_heads, axis=1)
    own_columns = lax.dynamic_slice_in_dim(summed_heads, tp_index * feature_count, feature_count, 1)
    normed = own_columns * lax.rsqrt(power / model_width + EPS)[:, None] * post_gain[None, :]
    residual_columns = lax.dynamic_slice_in_dim(
        hidden_in, tp_index * feature_count, feature_count, 1
    ).astype(jnp.float32)
    hidden_out = (residual_columns + normed).astype(jnp.bfloat16)
    leaf_onehot = (accepted_leaf[:, None] == jnp.arange(draft, dtype=jnp.int32)[None, :]).astype(
        jnp.float32
    )
    on_path = jnp.einsum("ri,rij->rj", leaf_onehot, ancestors, precision=lax.Precision.HIGHEST)
    target = cache_lengths[:, None] + tree_depth.astype(jnp.int32)
    placing = (places[None, :, None] == target[:, None, :]) & (on_path[:, None, :] > 0.5)
    written = jnp.any(placing, axis=-1)[..., None]
    placing_half = placing.astype(jnp.bfloat16)
    fresh_keys = jnp.einsum(
        "rpj,rjw->rpw",
        placing_half,
        keys.reshape(requests, draft, local_width),
        preferred_element_type=jnp.float32,
    ).astype(jnp.bfloat16)
    fresh_values = jnp.einsum(
        "rpj,rjw->rpw",
        placing_half,
        values.reshape(requests, draft, local_width),
        preferred_element_type=jnp.float32,
    ).astype(jnp.bfloat16)
    new_key_cache = jnp.where(written, fresh_keys, key_cache)
    new_value_cache = jnp.where(written, fresh_values, value_cache)
    return (hidden_out, new_key_cache, new_value_cache)


def solution(mesh):
    return jax.shard_map(
        body,
        mesh=mesh,
        in_specs=(
            P("seq", None),
            P(None, "tp"),
            P(None, "tp"),
            P(None, "tp"),
            P("tp", None),
            P("tp"),
            P("tp"),
            P("tp"),
            P(None, "seq", "tp"),
            P(None, "seq", "tp"),
            P(),
            P(),
            P(),
        ),
        out_specs=(P("seq", "tp"), P(None, "seq", "tp"), P(None, "seq", "tp")),
        check_vma=False,
    )
```

profile of v0, /device:TPU:2, one launch (start us, length us, event | category | flops | bytes accessed | tf_op | source)
XLA Modules:
  0.0 472.4 jit_solution(13318958439840656037)
XLA Ops:
  12.0 77.2 %all-gather.6.cloned.1.call-done = bf16[64,4,2048]{2,1,0:T(4,128)(2,1)} async-done(((bf16[1,4,2048]{2,1,0:T(4,128)(2,1)}), bf16[64,4,2048]{2,1,0:T(4,128)(2,1)}) %all-gather.6.cloned.1.call-update) | async-done | bytes 1048592 | tf_op jit(solution)/shard_map/all_gather | solution.py:102
  90.6 2.1 multiply_reduce_fusion
  92.7 2.1 multiply_reduce_fusion.1
  94.8 10.6 %all-reduce = (f32[256]{0:T(256)S(1)}, f32[256]{0:T(256)S(1)}) all-reduce(f32[256]{0:T(256)} %get-tuple-element.217, f32[256]{0:T(256)} %get-tuple-element.219), channel_id=1, replica_groups=mesh['seq'=64,'tp'=4] {'tp'}, use_global_device_ids=true, to_apply=%region_1.0 | all-reduce | flops 512 | bytes 4096 | tf_op jit(solution)/shard_map/psum | solution.py:114
  114.3 2.6 convolution_convert_fusion.2
  122.6 42.5 %all_gather.14 = f32[64,256,4]{1,2,0:T(4,128)S(1)} all-gather(f32[1,256,4]{1,2,0:T(4,128)S(1)} %all_gather_reshape.10), channel_id=1, replica_groups=mesh['seq'=64,'tp'=4] {'seq'}, dimensions={0}, use_global_device_ids=true | all-gather | bytes 266240 | tf_op jit(solution)/shard_map/all_gather | solution.py:14
  165.1 43.0 %all_gather.13 = f32[64,256,4]{1,2,0:T(4,128)S(1)} all-gather(f32[1,256,4]{1,2,0:T(4,128)S(1)} %all_gather_reshape.9), channel_id=1, replica_groups=mesh['seq'=64,'tp'=4] {'seq'}, dimensions={0}, use_global_device_ids=true | all-gather | bytes 266240 | tf_op jit(solution)/shard_map/all_gather | solution.py:14
  211.1 2.2 fusion.4
  213.3 2.0 fusion.3
  215.3 34.8 %all-gather.4.cloned.1.call-done = f32[64,256,512]{2,1,0:T(8,128)} async-done(((f32[1,256,512]{2,1,0:T(8,128)}), f32[64,256,512]{2,1,0:T(8,128)}) %all-gather.4.cloned.1.call-update) | async-done | bytes 33554448 | tf_op jit(solution)/shard_map/all_gather | solution.py:14
  251.1 193.7 %while.19 = (s32[]{:T(128)}, f32[256,4]{0,1:T(4,128)S(1)}, f32[256,4]{0,1:T(4,128)S(1)}, f32[256,512]{1,0:T(8,128)S(1)}, f32[64,256,4]{1,2,0:T(4,128)}, /*index=...) while((s32[]{:T(128)}, f32[256,4]{0,1:T(4,128)S(1)}, ...), condition=%wide.region_6.7_spmd, body=%wide.region_5.6_spmd.sunk | while | flops 399365 | bytes 3727503 | solution.py:20
  252.8 1.4 fusion.87
  255.9 1.4 fusion.87
  259.0 1.4 fusion.87
  262.0 1.4 fusion.87
  265.1 1.4 fusion.87
  268.2 1.4 fusion.87
  271.2 1.4 fusion.87
  274.3 1.4 fusion.87
  277.4 1.4 fusion.87
  280.5 1.4 fusion.87
  283.5 1.4 fusion.87
  286.6 1.4 fusion.87
  289.7 1.4 fusion.87
  292.7 1.4 fusion.87
  295.8 1.4 fusion.87
  298.9 1.4 fusion.87
  302.0 1.4 fusion.87
  305.0 1.4 fusion.87
  308.1 1.4 fusion.87
  311.2 1.4 fusion.87
  314.2 1.4 fusion.87
  317.3 1.4 fusion.87
  320.4 1.4 fusion.87
  323.5 1.4 fusion.87
  326.5 1.4 fusion.87
  329.6 1.4 fusion.87
  332.7 1.4 fusion.87
  335.7 1.4 fusion.87
  338.8 1.4 fusion.87
  341.9 1.4 fusion.87
  344.9 1.4 fusion.87
  348.0 1.4 fusion.87
  351.2 1.4 fusion.87
  354.3 1.4 fusion.87
  357.3 1.4 fusion.87
  360.5 1.4 fusion.87
  363.5 1.4 fusion.87
  366.6 1.4 fusion.87
  369.7 1.4 fusion.87
  372.8 1.4 fusion.87
  375.9 1.4 fusion.87
  378.9 1.4 fusion.87
  382.0 1.4 fusion.87
  385.1 1.4 fusion.87
  391.2 1.4 fusion.87
  409.7 1.4 fusion.87
  415.8 1.4 fusion.87
  421.9 1.4 fusion.87
  425.0 1.4 fusion.87
  431.2 1.4 fusion.87
  443.4 1.4 fusion.87
  445.2 2.0 fusion.59
  447.2 16.9 %psum.23 = f32[4,2048]{1,0:T(4,128)S(1)} all-reduce(f32[4,2048]{1,0:T(4,128)S(1)} %fusion.59), channel_id=1, replica_groups=mesh['seq'=64,'tp'=4] {'tp'}, use_global_device_ids=true, to_apply=%region_11.12 | all-reduce | flops 8192 | bytes 65536 | tf_op jit(solution)/shard_map/psum | solution.py:179
  (444 shorter events, 147.1 us)
Async XLA Ops:
  7.2 83.4 %copy-start = (bf16[2048,512]{1,0:T(8,128)(2,1)S(1)}, bf16[2048,512]{1,0:T(8,128)(2,1)}, u32[]{:S(2)}) copy-start(bf16[2048,512]{1,0:T(8,128)(2,1)} %param.17) | copy-start | bytes 6291460
  7.2 4.2 copy-start.23
  7.2 82.0 %all-gather.6.cloned.1.call-start = ((), (), s32[]{:S(2)}) async-start(), calls=%async_computation.1 | async-start | bytes 1064960 | tf_op jit(solution)/shard_map/all_gather | solution.py:102
  7.9 242.1 %all-gather.4.cloned.1.call-start = ((), (), s32[]{:S(2)}) async-start(), calls=%async_computation | async-start | bytes 34078720 | tf_op jit(solution)/shard_map/all_gather | solution.py:14
  11.4 81.3 %copy-start.15 = (s32[128]{0:T(128)}, s32[128]{0:T(128)S(1)}, u32[]{:S(2)}) copy-start(s32[128]{0:T(128)S(1)} %iota_add_fusion) | copy-start | bytes 1540
  11.5 97.4 %copy-start.21 = (pred[4,128]{1,0:T(4,128)(4,1)}, pred[4,128]{1,0:T(4,128)(4,1)S(1)}, u32[]{:S(2)}) copy-start(pred[4,128]{1,0:T(4,128)(4,1)S(1)} %broadcast_compare_fusion.1) | copy-start | bytes 1540
  90.6 4.2 copy-start.5
  90.6 2.2 copy-start.25
  92.7 13.2 %copy-start.19 = (f32[512]{0:T(512)S(1)}, f32[512]{0:T(512)}, u32[]{:S(2)}) copy-start(f32[512]{0:T(512)} %param.20) | copy-start | bytes 6148
  107.3 1.0 copy-start.7
  107.6 1.3 copy-start.1
  108.9 0.8 copy-start.3
  108.9 2.8 copy-start.26
  108.9 3.0 copy-start.24
  108.9 3.1 copy-start.16
  112.0 4.9 %copy-start.13 = (pred[4,64]{1,0:T(4,128)(4,1)}, pred[4,64]{1,0:T(4,128)(4,1)S(1)}, u32[]{:S(2)}) copy-start(pred[4,64]{1,0:T(4,128)(4,1)S(1)} %broadcast_compare_fusion) | copy-start | bytes 772
  113.7 4.0 copy-start.6
  113.7 4.0 copy-start.18
  113.7 4.0 copy-start.20
  116.9 0.7 copy-start.9
  118.3 3.2 copy-start.4
  118.4 92.6 %copy-start.2 = (bf16[4,128,512]{2,1,0:T(8,128)(2,1)S(1)}, bf16[4,128,512]{2,1,0:T(8,128)(2,1)}, u32[]{:S(2)}) copy-start(bf16[4,128,512]{2,1,0:T(8,128)(2,1)} %param.24) | copy-start | bytes 1572868
  118.5 92.6 %copy-start.14 = (pred[4,64]{1,0:T(4,128)(4,1)S(1)}, pred[4,64]{1,0:T(4,128)(4,1)}, u32[]{:S(2)}) copy-start(pred[4,64]{1,0:T(4,128)(4,1)} %copy-done.13) | copy-start | bytes 772
  122.5 90.8 %copy-start.8 = (bf16[4,128,512]{2,1,0:T(8,128)(2,1)S(1)}, bf16[4,128,512]{2,1,0:T(8,128)(2,1)}, u32[]{:S(2)}) copy-start(bf16[4,128,512]{2,1,0:T(8,128)(2,1)} %param.23) | copy-start | bytes 1572868
  165.1 46.0 %copy-start.10 = (f32[64,256,4]{1,2,0:T(4,128)}, f32[64,256,4]{1,2,0:T(4,128)S(1)}, u32[]{:S(2)}) copy-start(f32[64,256,4]{1,2,0:T(4,128)S(1)} %all_gather.14) | copy-start | bytes 786436
  208.1 2.9 copy-start.11
  251.1 193.8 %copy-start.12 = (bf16[64,4,128]{2,1,0:T(4,128)(2,1)S(1)}, bf16[64,4,128]{2,1,0:T(4,128)(2,1)}, u32[]{:S(2)}) copy-start(bf16[64,4,128]{2,1,0:T(4,128)(2,1)} %reshape.240) | copy-start | bytes 196612
  251.1 193.8 %copy-start.17 = (pred[4,64]{1,0:T(4,128)(4,1)S(1)}, pred[4,64]{1,0:T(4,128)(4,1)}, u32[]{:S(2)}) copy-start(pred[4,64]{1,0:T(4,128)(4,1)} %fusion.43) | copy-start | bytes 772
  444.8 19.3 %copy-start.22 = (f32[512]{0:T(512)S(1)}, f32[512]{0:T(512)}, u32[]{:S(2)}) copy-start(f32[512]{0:T(512)} %param.22) | copy-start | bytes 6148
Sparse Core Ops, SparseCore 0:
  10.8 78.3 all-gather.5
  111.2 138.7 all-gather.3
where the time goes:
time: 478 us; the launch traced here: 472 us
  other arithmetic  141 us (29%)
  waiting for transfers between devices  113 us (24%)
  blocking collectives  113 us (24%)
  local copies, waits for them, and re-layouts  71 us (15%)
  matrix products  17.9 us (4%)
  between operations  14.6 us (3%)
    add x63, other arithmetic, join_partials(): out_first.reshape(rows_here, heads_here, -1) * scale_first[..., None]  87 us
    all_gather x2, blocking collectives, joined_2(): everything = jax.tree.map(lambda part: lax.all_gather(part, axis), x)  85.5 us
    all_gather x1, waiting for transfers between devices, body(): piece = lax.all_gather(hidden_in, 'seq', axis=0, tiled=True)  77.2 us
    add x64, other arithmetic, join_partials(): total_first * scale_first + total_second * scale_second  45 us
    all_gather x1, waiting for transfers between devices, joined_2(): everything = jax.tree.map(lambda part: lax.all_gather(part, axis), x)  34.8 us
    mul x63, local copies, waits for them, and re-layouts, join_partials(): out_first.reshape(rows_here, heads_here, -1) * scale_first[..., None]  21.1 us
    mul x63, local copies, waits for them, and re-layouts, join_partials(): out_second.reshape(rows_here, heads_here, -1) * scale_second[..., None]  21.1 us
    psum x1, blocking collectives, body(): summed_heads = lax.psum(projected, 'tp')  16.9 us
  transfers between devices with their start and end apart: 2, of which 2 were waited for; matrix products, arithmetic and copies ran while one was open for 5% of the time, Pallas kernels for 0%

commit v1 on v0

--- a/solution.py
+++ b/solution.py
@@ -99,7 +99,9 @@
     row_start = seq_index * own_rows
     ancestors, tree_depth = ancestry(parents)
     positions = (cache_lengths[:, None].astype(jnp.float32) + tree_depth).reshape(tokens)
-    piece = lax.all_gather(hidden_in, "seq", axis=0, tiled=True)
+    piece = jnp.concatenate(
+        lax.all_to_all(jnp.stack([hidden_in] * lax.axis_size("seq")), "seq", 0, 0), axis=0
+    )
     raw = jnp.concatenate(
         [
             jnp.dot(piece, query_weight, preferred_element_type=jnp.float32),

time: 478 us -> 435 us (0.910)
  waiting for transfers between devices: 113 us -> 58.9 us
  starting transfers between devices: 0.08 us -> 12.1 us
    all_gather x1 -> x0, waiting for transfers between devices: 77.2 us -> none  [body(): piece = lax.all_gather(hidden_in, 'seq', axis=0, tiled=True)]
    all_to_all x0 -> x1, waiting for transfers between devices: none -> 24.5 us  [body(): lax.all_to_all(jnp.stack([hidden_in] * lax.axis_size('seq')), 'seq', 0, 0)]
    all_to_all x0 -> x1, starting transfers between devices: none -> 12 us  [body(): lax.all_to_all(jnp.stack([hidden_in] * lax.axis_size('seq')), 'seq', 0, 0)]
where the time goes in v1:
time: 435 us; the launch traced here: 430 us
  other arithmetic  139 us (32%)
  blocking collectives  113 us (26%)
  local copies, waits for them, and re-layouts  73.1 us (17%)
  waiting for transfers between devices  58.9 us (14%)
  matrix products  16.7 us (4%)
  between operations  14.6 us (3%)
  starting transfers between devices  12.1 us (3%)
    add x63, other arithmetic, join_partials(): out_first.reshape(rows_here, heads_here, -1) * scale_first[..., None]  87 us
    all_gather x2, blocking collectives, joined_2(): everything = jax.tree.map(lambda part: lax.all_gather(part, axis), x)  85.3 us
    add x64, other arithmetic, join_partials(): total_first * scale_first + total_second * scale_second  45 us
    all_gather x1, waiting for transfers between devices, joined_2(): everything = jax.tree.map(lambda part: lax.all_gather(part, axis), x)  34.4 us
    all_to_all x1, waiting for transfers between devices, body(): lax.all_to_all(jnp.stack([hidden_in] * lax.axis_size('seq')), 'seq', 0, 0)  24.5 us
    mul x63, local copies, waits for them, and re-layouts, join_partials(): out_first.reshape(rows_here, heads_here, -1) * scale_first[..., None]  21.1 us
    mul x63, local copies, waits for them, and re-layouts, join_partials(): out_second.reshape(rows_here, heads_here, -1) * scale_second[..., None]  21.1 us
    psum x1, blocking collectives, body(): summed_heads = lax.psum(projected, 'tp')  16.9 us
  transfers between devices with their start and end apart: 2, of which 2 were waited for; matrix products, arithmetic and copies ran while one was open for 5% of the time, Pallas kernels for 0%

profile of v1, /device:TPU:2, one launch (start us, length us, event | category | flops | bytes accessed | tf_op | source)
XLA Modules:
  0.0 429.6 jit_solution(12594305683040543119)
XLA Ops:
  7.2 2.4 stack.2
  9.6 12.0 %all-to-all-start = ((bf16[64,4,2048]{2,1,0:T(4,128)(2,1)}), bf16[64,4,2048]{2,1,0:T(4,128)(2,1)S(1)}, u32[]{:S(2)}, u32[]{:S(2)}) async-start(bf16[64,4,2048]{2,1,0:T(4,128)(2,1)} %stack.2), calls=%async_computation | async-start | bytes 2097152 | tf_op jit(solution)/shard_map/all_to_all | solution.py:103
  24.3 24.5 %all-to-all-done = bf16[64,4,2048]{2,1,0:T(4,128)(2,1)S(1)} async-done(((bf16[64,4,2048]{2,1,0:T(4,128)(2,1)}), bf16[64,4,2048]{2,1,0:T(4,128)(2,1)S(1)}, u32[]{:S(2)}, u32[]{:S(2)}) %all-to-all-start) | async-done | bytes 1048608 | tf_op jit(solution)/shard_map/all_to_all | solution.py:103
  49.8 2.9 multiply_reduce_fusion
  53.5 10.7 %all-reduce = (f32[256]{0:T(256)S(1)}, f32[256]{0:T(256)S(1)}) all-reduce(f32[256]{0:T(256)S(1)} %get-tuple-element.217, f32[256]{0:T(256)S(1)} %get-tuple-element.219), channel_id=1, replica_groups=mesh['seq'=64,'tp'=4] {'tp'}, use_global_device_ids=true, to_apply=%region_1.0 | all-reduce | flops 512 | bytes 4096 | tf_op jit(solution)/shard_map/psum | solution.py:116
  72.1 2.6 convolution_convert_fusion.2
  80.5 42.9 %all_gather.10 = f32[64,256,4]{1,2,0:T(4,128)S(1)} all-gather(f32[1,256,4]{1,2,0:T(4,128)S(1)} %all_gather_reshape.10), channel_id=1, replica_groups=mesh['seq'=64,'tp'=4] {'seq'}, dimensions={0}, use_global_device_ids=true | all-gather | bytes 266240 | tf_op jit(solution)/shard_map/all_gather | solution.py:14
  123.4 42.3 %all_gather.9 = f32[64,256,4]{1,2,0:T(4,128)S(1)} all-gather(f32[1,256,4]{1,2,0:T(4,128)S(1)} %all_gather_reshape.9), channel_id=1, replica_groups=mesh['seq'=64,'tp'=4] {'seq'}, dimensions={0}, use_global_device_ids=true | all-gather | bytes 266240 | tf_op jit(solution)/shard_map/all_gather | solution.py:14
  168.7 2.2 fusion.4
  171.0 2.0 fusion.3
  172.9 34.4 %all-gather.2.cloned.1.call-done = f32[64,256,512]{2,1,0:T(8,128)} async-done(((f32[1,256,512]{2,1,0:T(8,128)}), f32[64,256,512]{2,1,0:T(8,128)}) %all-gather.2.cloned.1.call-update) | async-done | bytes 33554448 | tf_op jit(solution)/shard_map/all_gather | solution.py:14
  208.4 193.7 %while.19 = (s32[]{:T(128)}, f32[256,4]{0,1:T(4,128)S(1)}, f32[256,4]{0,1:T(4,128)S(1)}, f32[256,512]{1,0:T(8,128)S(1)}, f32[64,256,4]{1,2,0:T(4,128)}, /*index=...) while((s32[]{:T(128)}, f32[256,4]{0,1:T(4,128)S(1)}, ...), condition=%wide.region_6.7_spmd, body=%wide.region_5.6_spmd.sunk | while | flops 399365 | bytes 3727503 | solution.py:20
  210.1 1.4 fusion.87
  213.1 1.4 fusion.87
  216.2 1.4 fusion.87
  219.3 1.4 fusion.87
  222.4 1.4 fusion.87
  225.4 1.4 fusion.87
  228.5 1.4 fusion.87
  231.6 1.4 fusion.87
  234.6 1.4 fusion.87
  237.7 1.4 fusion.87
  240.8 1.4 fusion.87
  243.9 1.4 fusion.87
  246.9 1.4 fusion.87
  250.0 1.4 fusion.87
  253.1 1.4 fusion.87
  256.1 1.4 fusion.87
  259.2 1.4 fusion.87
  262.3 1.4 fusion.87
  265.4 1.4 fusion.87
  268.4 1.4 fusion.87
  271.5 1.4 fusion.87
  274.6 1.4 fusion.87
  277.6 1.4 fusion.87
  280.7 1.4 fusion.87
  283.8 1.4 fusion.87
  286.9 1.4 fusion.87
  289.9 1.4 fusion.87
  293.0 1.4 fusion.87
  296.1 1.4 fusion.87
  299.1 1.4 fusion.87
  302.2 1.4 fusion.87
  305.3 1.4 fusion.87
  308.4 1.4 fusion.87
  311.5 1.4 fusion.87
  314.6 1.4 fusion.87
  317.7 1.4 fusion.87
  320.8 1.4 fusion.87
  323.9 1.4 fusion.87
  327.0 1.4 fusion.87
  330.1 1.4 fusion.87
  333.1 1.4 fusion.87
  336.2 1.4 fusion.87
  339.3 1.4 fusion.87
  342.3 1.4 fusion.87
  345.4 1.4 fusion.87
  348.5 1.4 fusion.87
  363.8 1.4 fusion.87
  385.3 1.4 fusion.87
  391.5 1.4 fusion.87
  394.6 1.4 fusion.87
  402.4 2.0 fusion.59
  404.4 16.9 %psum.23 = f32[4,2048]{1,0:T(4,128)S(1)} all-reduce(f32[4,2048]{1,0:T(4,128)S(1)} %fusion.59), channel_id=1, replica_groups=mesh['seq'=64,'tp'=4] {'tp'}, use_global_device_ids=true, to_apply=%region_11.12 | all-reduce | flops 8192 | bytes 65536 | tf_op jit(solution)/shard_map/psum | solution.py:181
  (446 shorter events, 145.8 us)
Async XLA Ops:
  7.2 42.7 %copy-start = (bf16[2048,512]{1,0:T(8,128)(2,1)S(1)}, bf16[2048,512]{1,0:T(8,128)(2,1)}, u32[]{:S(2)}) copy-start(bf16[2048,512]{1,0:T(8,128)(2,1)} %param.17) | copy-start | bytes 6291460
  7.2 14.5 %copy-start.24 = (s32[4]{0:T(128)S(1)}, s32[4]{0:T(128)}, u32[]{:S(2)}) copy-start(s32[4]{0:T(128)} %param.25) | copy-start | bytes 52
  7.2 14.5 %copy-start.23 = (s32[4,64]{1,0:T(4,128)S(1)}, s32[4,64]{1,0:T(4,128)}, u32[]{:S(2)}) copy-start(s32[4,64]{1,0:T(4,128)} %param.26) | copy-start | bytes 3076
  9.6 39.2 %all-to-all-start = ((bf16[64,4,2048]{2,1,0:T(4,128)(2,1)}), bf16[64,4,2048]{2,1,0:T(4,128)(2,1)S(1)}, u32[]{:S(2)}, u32[]{:S(2)}) async-start(bf16[64,4,2048]{2,1,0:T(4,128)(2,1)} %stack.2), calls=%async_computation | async-start | bytes 2097152 | tf_op jit(solution)/shard_map/all_to_all | solution.py:103
  21.6 185.7 %all-gather.2.cloned.1.call-start = ((), (), s32[]{:S(2)}) async-start(), calls=%async_computation.1 | async-start | bytes 34078720 | tf_op jit(solution)/shard_map/all_gather | solution.py:14
  23.6 29.1 %copy-start.15 = (s32[128]{0:T(128)}, s32[128]{0:T(128)S(1)}, u32[]{:S(2)}) copy-start(s32[128]{0:T(128)S(1)} %iota_add_fusion) | copy-start | bytes 1540
  23.7 43.0 %copy-start.21 = (pred[4,128]{1,0:T(4,128)(4,1)}, pred[4,128]{1,0:T(4,128)(4,1)S(1)}, u32[]{:S(2)}) copy-start(pred[4,128]{1,0:T(4,128)(4,1)S(1)} %broadcast_compare_fusion.1) | copy-start | bytes 1540
  49.8 2.9 copy-start.5
  49.8 2.9 copy-start.26
  52.7 12.1 %copy-start.19 = (f32[512]{0:T(512)S(1)}, f32[512]{0:T(512)}, u32[]{:S(2)}) copy-start(f32[512]{0:T(512)} %param.20) | copy-start | bytes 6148
  65.1 1.0 copy-start.7
  65.5 1.3 copy-start.1
  66.7 0.8 copy-start.3
  66.8 2.8 copy-start.27
  66.8 3.0 copy-start.25
  66.8 3.1 copy-start.16
  69.8 4.9 %copy-start.13 = (pred[4,64]{1,0:T(4,128)(4,1)}, pred[4,64]{1,0:T(4,128)(4,1)S(1)}, u32[]{:S(2)}) copy-start(pred[4,64]{1,0:T(4,128)(4,1)S(1)} %broadcast_compare_fusion) | copy-start | bytes 772
  71.5 4.0 copy-start.6
  71.5 4.0 copy-start.18
  71.5 4.0 copy-start.20
  74.8 0.7 copy-start.9
  76.1 3.1 copy-start.4
  76.3 92.4 %copy-start.2 = (bf16[4,128,512]{2,1,0:T(8,128)(2,1)S(1)}, bf16[4,128,512]{2,1,0:T(8,128)(2,1)}, u32[]{:S(2)}) copy-start(bf16[4,128,512]{2,1,0:T(8,128)(2,1)} %param.24) | copy-start | bytes 1572868
  76.3 92.4 %copy-start.14 = (pred[4,64]{1,0:T(4,128)(4,1)S(1)}, pred[4,64]{1,0:T(4,128)(4,1)}, u32[]{:S(2)}) copy-start(pred[4,64]{1,0:T(4,128)(4,1)} %copy-done.13) | copy-start | bytes 772
  80.4 90.6 %copy-start.8 = (bf16[4,128,512]{2,1,0:T(8,128)(2,1)S(1)}, bf16[4,128,512]{2,1,0:T(8,128)(2,1)}, u32[]{:S(2)}) copy-start(bf16[4,128,512]{2,1,0:T(8,128)(2,1)} %param.23) | copy-start | bytes 1572868
  123.4 45.3 %copy-start.10 = (f32[64,256,4]{1,2,0:T(4,128)}, f32[64,256,4]{1,2,0:T(4,128)S(1)}, u32[]{:S(2)}) copy-start(f32[64,256,4]{1,2,0:T(4,128)S(1)} %all_gather.10) | copy-start | bytes 786436
  165.7 2.9 copy-start.11
  208.4 193.8 %copy-start.12 = (bf16[64,4,128]{2,1,0:T(4,128)(2,1)S(1)}, bf16[64,4,128]{2,1,0:T(4,128)(2,1)}, u32[]{:S(2)}) copy-start(bf16[64,4,128]{2,1,0:T(4,128)(2,1)} %reshape.246) | copy-start | bytes 196612
  208.4 193.8 %copy-start.17 = (pred[4,64]{1,0:T(4,128)(4,1)S(1)}, pred[4,64]{1,0:T(4,128)(4,1)}, u32[]{:S(2)}) copy-start(pred[4,64]{1,0:T(4,128)(4,1)} %fusion.43) | copy-start | bytes 772
  402.1 19.3 %copy-start.22 = (f32[512]{0:T(512)S(1)}, f32[512]{0:T(512)}, u32[]{:S(2)}) copy-start(f32[512]{0:T(512)} %param.22) | copy-start | bytes 6148
Sparse Core Ops, SparseCore 0:
  69.1 138.1 all-gather.1
